TPU v7x, 128 devices: a whole 4x4x4 slice. The times are simulated.
128 devices in a mesh: row: 32 (over z, x, y_lo), ch: 4 (over y_hi, core).
Axes of the slice: x: 4, y: 4 (y_hi: 2, y_lo: 2; y = y_hi * 2 + y_lo), z: 4, core: 2. Of those that a mesh axis runs over, the one named last changes fastest.
Arguments:
- pair_in: bfloat16 [512, 512, 128], P('row', 'ch'), may hold values from -6 to 6
- grad_out: bfloat16 [512, 512, 128], P('row', 'ch'), may hold values from -6 to 6
- token_valid: int32 [512], replicated, may hold values from 0 to 1, as said below
- chain_ids: int32 [512], replicated, may hold values from 0 to 7, never falling along the last dimension, each value on 1 to 128 neighbouring positions
- chain_table: float32 [2, 128], replicated, may hold values from -4 to 4
- norm_gain: float32 [2, 2, 128], replicated, may hold values from 0.1 to 1.9
- norm_offset: float32 [2, 2, 128], replicated, may hold values from -3 to 3
- proj_in: bfloat16 [2, 128, 640], replicated, may hold values from -0.5 to 0.5
- proj_out: bfloat16 [2, 128, 128], replicated, may hold values from -0.5 to 0.5
Outputs:
- final_pair: bfloat16 [512, 512, 128], P('row', 'ch')
- pair_grad: bfloat16 [512, 512, 128], P('row', 'ch')
Inputs may be any that keep to these rules, and one draw needn't show every extreme that they name: token_valid is 1 on a leading run of at least 256 tokens and 0 on the rest; the last token is always padding. `chain_ids`: chain ids never fall along the crop.
All inputs are finite; a program needn't handle non-finite values.
Results may differ from a plain program's by a relative error of at most 0.0075.
Values may be sent and summed in bfloat16 or wider, within the bound.
A program may use at most 128 MiB of HBM per device.

v0:
```python
import jax
import jax.numpy as jnp
from jax import lax
from jax.sharding import PartitionSpec as P

EPS = 1e-05


def layer_norm(values, norm_scale, norm_shift, along):
    average = jnp.mean(values, axis=along, keepdims=True)
    centred = values - average
    spread = jnp.mean(centred * centred, axis=along, keepdims=True)
    return centred * lax.rsqrt(spread + EPS) * norm_scale + norm_shift


def gated(linear):
    gate_part, value_part = jnp.split(linear, 2, axis=0)
    return jax.nn.sigmoid(gate_part) * value_part


def gated_back(linear, upstream):
    gate_part, value_part = jnp.split(linear, 2, axis=0)
    squash = jax.nn.sigmoid(gate_part)
    return jnp.concatenate(
        [upstream * value_part * squash * (1.0 - squash), upstream * squash], axis=0
    )


def from_blocks(received, row_count, col_count):
    blocks, row_len, col_len = received.shape
    per_dev = blocks // (row_count * col_count)
    shaped = received.reshape(row_count, col_count, per_dev, row_len, col_len)
    return shaped.transpose(2, 0, 3, 1, 4).reshape(
        per_dev, row_count * row_len, col_count * col_len
    )


def to_blocks(channels, row_count, col_count):
    per_dev, total_rows, total_cols = channels.shape
    shaped = channels.reshape(
        per_dev, row_count, total_rows // row_count, col_count, total_cols // col_count
    )
    return shaped.transpose(1, 3, 0, 2, 4).reshape(
        row_count * col_count * per_dev, total_rows // row_count, total_cols // col_count
    )


def spread_factors(left_factor, right_factor):
    row_count = lax.axis_size("row")
    col_count = lax.axis_size("ch")
    moved_pieces = (
        lax.all_to_all(left_factor, ("row", "ch"), split_axis=0, concat_axis=0, tiled=True),
        lax.all_to_all(right_factor, ("row", "ch"), split_axis=0, concat_axis=0, tiled=True),
    )
    return tuple((from_blocks(one_piece, row_count, col_count) for one_piece in moved_pieces))


def spread_cotangent(grad_tri):
    row_count = lax.axis_size("row")
    col_count = lax.axis_size("ch")
    moved_piece = lax.all_to_all(grad_tri, ("row", "ch"), split_axis=0, concat_axis=0, tiled=True)
    return from_blocks(moved_piece, row_count, col_count)


def collect_product(product):
    row_count = lax.axis_size("row")
    col_count = lax.axis_size("ch")
    return lax.all_to_all(
        to_blocks(product, row_count, col_count),
        ("row", "ch"),
        split_axis=0,
        concat_axis=0,
        tiled=True,
    )


def collect_grads(grad_left, grad_right):
    row_count = lax.axis_size("row")
    col_count = lax.axis_size("ch")
    return (
        lax.all_to_all(
            to_blocks(grad_left, row_count, col_count),
            ("row", "ch"),
            split_axis=0,
            concat_axis=0,
            tiled=True,
        ),
        lax.all_to_all(
            to_blocks(grad_right, row_count, col_count),
            ("row", "ch"),
            split_axis=0,
            concat_axis=0,
            tiled=True,
        ),
    )


def batched_dot(first, second, first_dim, second_dim):
    return lax.dot_general(
        first,
        second,
        (((first_dim,), (second_dim,)), ((0,), (0,))),
        preferred_element_type=jnp.float32,
    )


def forward_block(block_in, pair_mask, gains, offsets, weight_in, weight_out, outgoing):
    pair_width = weight_in.shape[0]
    input32 = block_in.astype(jnp.float32)
    normed = layer_norm(input32, gains[0], offsets[0], 2).astype(jnp.bfloat16)
    lin_left = jnp.einsum(
        "ijc,cd->dij", normed, weight_in[:, : 2 * pair_width], preferred_element_type=jnp.float32
    )
    lin_right = jnp.einsum(
        "ijc,cd->dij",
        normed,
        weight_in[:, 2 * pair_width : 4 * pair_width],
        preferred_element_type=jnp.float32,
    )
    lin_gate = jnp.dot(normed, weight_in[:, 4 * pair_width :], preferred_element_type=jnp.float32)
    left_factor = (pair_mask * gated(lin_left)).astype(jnp.bfloat16)
    right_factor = (pair_mask * gated(lin_right)).astype(jnp.bfloat16)
    gate_value = jax.nn.sigmoid(lin_gate)
    left_channels, right_channels = spread_factors(left_factor, right_factor)
    if outgoing:
        product = batched_dot(left_channels, right_channels, 2, 2)
    else:
        product = batched_dot(left_channels, right_channels, 1, 1)
    triangle = collect_product(product.astype(jnp.bfloat16))
    gain_col = gains[1][:, None, None]
    offset_col = offsets[1][:, None, None]
    tri_norm = layer_norm(triangle.astype(jnp.float32), gain_col, offset_col, 0).astype(
        jnp.bfloat16
    )
    mixed_out = jnp.einsum("cij,cd->ijd", tri_norm, weight_out, preferred_element_type=jnp.float32)
    block_out = (input32 + gate_value * mixed_out).astype(jnp.bfloat16)
    held_factors = (left_channels, right_channels)
    return (
        block_out,
        (input32, lin_left, lin_right, gate_value, held_factors, triangle, mixed_out),
    )


def backward_block(grad_in, saved, pair_mask, gains, offsets, weight_in, weight_out, outgoing):
    input32, lin_left, lin_right, gate_value, held_factors, triangle, mixed_out = saved
    pair_width = weight_in.shape[0]
    upstream = grad_in.astype(jnp.float32)
    grad_gate = upstream * mixed_out
    grad_mixed = (upstream * gate_value).astype(jnp.bfloat16)
    grad_tnorm = jnp.einsum(
        "ijd,cd->cij", grad_mixed, weight_out, preferred_element_type=jnp.float32
    )
    gain_col = gains[1][:, None, None]
    offset_col = offsets[1][:, None, None]
    _, out_back = jax.vjp(
        lambda values: layer_norm(values, gain_col, offset_col, 0), triangle.astype(jnp.float32)
    )
    grad_tri = out_back(grad_tnorm)[0].astype(jnp.bfloat16)
    grad_channels = spread_cotangent(grad_tri)
    left_channels, right_channels = held_factors
    if outgoing:
        grad_left_ch = batched_dot(grad_channels, right_channels, 2, 1)
        grad_right_ch = batched_dot(grad_channels, left_channels, 1, 1)
    else:
        grad_left_ch = batched_dot(right_channels, grad_channels, 2, 2)
        grad_right_ch = batched_dot(left_channels, grad_channels, 2, 1)
    grad_left, grad_right = collect_grads(
        grad_left_ch.astype(jnp.bfloat16), grad_right_ch.astype(jnp.bfloat16)
    )
    grad_lin_left = gated_back(lin_left, pair_mask * grad_left.astype(jnp.float32)).astype(
        jnp.bfloat16
    )
    grad_lin_right = gated_back(lin_right, pair_mask * grad_right.astype(jnp.float32)).astype(
        jnp.bfloat16
    )
    grad_lin_gate = (grad_gate * gate_value * (1.0 - gate_value)).astype(jnp.bfloat16)
    grad_normed = (
        jnp.einsum(
            "dij,cd->ijc",
            grad_lin_left,
            weight_in[:, : 2 * pair_width],
            preferred_element_type=jnp.float32,
        )
        + jnp.einsum(
            "dij,cd->ijc",
            grad_lin_right,
            weight_in[:, 2 * pair_width : 4 * pair_width],
            preferred_element_type=jnp.float32,
        )
        + jnp.dot(
            grad_lin_gate, weight_in[:, 4 * pair_width :].T, preferred_element_type=jnp.float32
        )
    )
    _, in_back = jax.vjp(lambda values: layer_norm(values, gains[0], offsets[0], 2), input32)
    return (upstream + in_back(grad_normed)[0]).astype(jnp.bfloat16)


def local(
    pair_in,
    grad_out,
    token_valid,
    chain_ids,
    chain_table,
    norm_gain,
    norm_offset,
    proj_in,
    proj_out,
):
    row_len, col_len, pair_width = pair_in.shape
    row_start = lax.axis_index("row") * row_len
    col_start = lax.axis_index("ch") * col_len
    valid_rows = lax.dynamic_slice_in_dim(token_valid, row_start, row_len).astype(jnp.float32)
    valid_cols = lax.dynamic_slice_in_dim(token_valid, col_start, col_len).astype(jnp.float32)
    pair_mask = valid_rows[:, None] * valid_cols[None, :]
    chain_rows = lax.dynamic_slice_in_dim(chain_ids, row_start, row_len)
    chain_cols = lax.dynamic_slice_in_dim(chain_ids, col_start, col_len)
    same_chain = (chain_rows[:, None] == chain_cols[None, :]).astype(jnp.float32)[:, :, None]
    entry_pair = (
        pair_in.astype(jnp.float32)
        + same_chain * chain_table[1]
        + (1.0 - same_chain) * chain_table[0]
    ).astype(jnp.bfloat16)
    middle, first_saved = forward_block(
        entry_pair, pair_mask, norm_gain[0], norm_offset[0], proj_in[0], proj_out[0], True
    )
    final_pair, second_saved = forward_block(
        middle, pair_mask, norm_gain[1], norm_offset[1], proj_in[1], proj_out[1], False
    )
    grad_middle = backward_block(
        grad_out,
        second_saved,
        pair_mask,
        norm_gain[1],
        norm_offset[1],
        proj_in[1],
        proj_out[1],
        False,
    )
    pair_grad = backward_block(
        grad_middle,
        first_saved,
        pair_mask,
        norm_gain[0],
        norm_offset[0],
        proj_in[0],
        proj_out[0],
        True,
    )
    return (final_pair, pair_grad)


def solution(mesh):
    in_specs = (P("row", "ch", None), P("row", "ch", None), P(), P(), P(), P(), P(), P(), P())
    out_specs = (P("row", "ch", None), P("row", "ch", None))
    return jax.shard_map(local, mesh=mesh, in_specs=in_specs, out_specs=out_specs, check_vma=False)
```

profile of v0, /device:TPU:1, one launch (start us, length us, event | category | flops | bytes accessed | tf_op | source)
XLA Modules:
  0.0 278.6 jit_solution(11534861614545217164)
XLA Ops:
  12.0 11.5 %all-to-all-start = ((bf16[128,16,128]{2,1,0:T(8,128)(2,1)}), bf16[128,16,128]{2,1,0:T(8,128)(2,1)S(1)}, u32[]{:S(2)}, u32[]{:S(2)}) async-start(bf16[128,16,128]{2,1,0:T(8,128)(2,1)} %copy.102), calls=%async_computation | async-start | bytes 1048576 | tf_op jit(solution)/shard_map/all_to_all | solution.py:52
  24.7 12.6 %all-to-all-done = bf16[128,16,128]{2,1,0:T(8,128)(2,1)S(1)} async-done(((bf16[128,16,128]{2,1,0:T(8,128)(2,1)}), bf16[128,16,128]{2,1,0:T(8,128)(2,1)S(1)}, u32[]{:S(2)}, u32[]{:S(2)}) %all-to-all-start) | async-done | bytes 524320 | tf_op jit(solution)/shard_map/all_to_all | solution.py:52
  37.3 4.2 %all-to-all-start.1 = ((bf16[128,16,128]{2,1,0:T(8,128)(2,1)}), bf16[128,16,128]{2,1,0:T(8,128)(2,1)S(1)}, u32[]{:S(2)}, u32[]{:S(2)}) async-start(bf16[128,16,128]{2,1,0:T(8,128)(2,1)} %copy.106), calls=%async_computation.1 | async-start | bytes 1048576 | tf_op jit(solution)/shard_map/all_to_all | solution.py:53
  41.8 13.7 %all-to-all-done.1 = bf16[128,16,128]{2,1,0:T(8,128)(2,1)S(1)} async-done(((bf16[128,16,128]{2,1,0:T(8,128)(2,1)}), bf16[128,16,128]{2,1,0:T(8,128)(2,1)S(1)}, u32[]{:S(2)}, u32[]{:S(2)}) %all-to-all-start.1) | async-done | bytes 524320 | tf_op jit(solution)/shard_map/all_to_all | solution.py:53
  56.4 17.5 %all_to_all.60 = bf16[128,16,128]{2,1,0:T(8,128)(2,1)S(1)} all-to-all(bf16[128,16,128]{2,1,0:T(8,128)(2,1)S(1)} %bitcast.169), channel_id=1, replica_groups=mesh['row'=32,'ch'=4] {'row','ch'}, dimensions={0} | all-to-all | bytes 1048576 | tf_op jit(solution)/shard_map/all_to_all | solution.py:68
  80.4 4.2 %all-to-all-start.3 = ((bf16[128,16,128]{2,1,0:T(8,128)(2,1)}), bf16[128,16,128]{2,1,0:T(8,128)(2,1)S(1)}, u32[]{:S(2)}, u32[]{:S(2)}) async-start(bf16[128,16,128]{2,1,0:T(8,128)(2,1)} %copy.114), calls=%async_computation.3 | async-start | bytes 1048576 | tf_op jit(solution)/shard_map/all_to_all | solution.py:52
  85.8 12.7 %all-to-all-done.3 = bf16[128,16,128]{2,1,0:T(8,128)(2,1)S(1)} async-done(((bf16[128,16,128]{2,1,0:T(8,128)(2,1)}), bf16[128,16,128]{2,1,0:T(8,128)(2,1)S(1)}, u32[]{:S(2)}, u32[]{:S(2)}) %all-to-all-start.3) | async-done | bytes 524320 | tf_op jit(solution)/shard_map/all_to_all | solution.py:52
  98.5 4.2 %all-to-all-start.4 = ((bf16[128,16,128]{2,1,0:T(8,128)(2,1)}), bf16[128,16,128]{2,1,0:T(8,128)(2,1)S(1)}, u32[]{:S(2)}, u32[]{:S(2)}) async-start(bf16[128,16,128]{2,1,0:T(8,128)(2,1)} %copy.117), calls=%async_computation.4 | async-start | bytes 1048576 | tf_op jit(solution)/shard_map/all_to_all | solution.py:53
  103.0 13.7 %all-to-all-done.4 = bf16[128,16,128]{2,1,0:T(8,128)(2,1)S(1)} async-done(((bf16[128,16,128]{2,1,0:T(8,128)(2,1)}), bf16[128,16,128]{2,1,0:T(8,128)(2,1)S(1)}, u32[]{:S(2)}, u32[]{:S(2)}) %all-to-all-start.4) | async-done | bytes 524320 | tf_op jit(solution)/shard_map/all_to_all | solution.py:53
  121.1 4.2 %all-to-all-start.5 = ((bf16[128,16,128]{2,1,0:T(8,128)(2,1)}), bf16[128,16,128]{2,1,0:T(8,128)(2,1)S(1)}, u32[]{:S(2)}, u32[]{:S(2)}) async-start(bf16[128,16,128]{2,1,0:T(8,128)(2,1)} %bitcast.33), calls=%async_computation.5 | async-start | bytes 1048576 | tf_op jit(solution)/shard_map/all_to_all | solution.py:68
  126.9 12.4 %all-to-all-done.5 = bf16[128,16,128]{2,1,0:T(8,128)(2,1)S(1)} async-done(((bf16[128,16,128]{2,1,0:T(8,128)(2,1)}), bf16[128,16,128]{2,1,0:T(8,128)(2,1)S(1)}, u32[]{:S(2)}, u32[]{:S(2)}) %all-to-all-start.5) | async-done | bytes 524320 | tf_op jit(solution)/shard_map/all_to_all | solution.py:68
  141.9 17.5 %all_to_all.61 = bf16[128,16,128]{2,1,0:T(8,128)(2,1)S(1)} all-to-all(bf16[128,16,128]{2,1,0:T(8,128)(2,1)S(1)} %copy.125), channel_id=1, replica_groups=mesh['row'=32,'ch'=4] {'row','ch'}, dimensions={0} | all-to-all | bytes 1048576 | tf_op jit(solution)/shard_map/all_to_all | solution.py:61
  165.6 5.3 %all-to-all-start.8 = ((bf16[128,16,128]{2,1,0:T(8,128)(2,1)}), bf16[128,16,128]{2,1,0:T(8,128)(2,1)}, u32[]{:S(2)}, u32[]{:S(2)}) async-start(bf16[128,16,128]{2,1,0:T(8,128)(2,1)} %bitcast.165), calls=%async_computation.8 | async-start | bytes 1048576 | tf_op jit(solution)/shard_map/all_to_all | solution.py:88
  170.8 2.5 convolution_convert_fusion.3
  177.3 7.1 %all-to-all-done.8 = bf16[128,16,128]{2,1,0:T(8,128)(2,1)} async-done(((bf16[128,16,128]{2,1,0:T(8,128)(2,1)}), bf16[128,16,128]{2,1,0:T(8,128)(2,1)}, u32[]{:S(2)}, u32[]{:S(2)}) %all-to-all-start.8) | async-done | bytes 524320 | tf_op jit(solution)/shard_map/all_to_all | solution.py:88
  184.4 5.3 %all-to-all-start.7 = ((bf16[128,16,128]{2,1,0:T(8,128)(2,1)}), bf16[128,16,128]{2,1,0:T(8,128)(2,1)}, u32[]{:S(2)}, u32[]{:S(2)}) async-start(bf16[128,16,128]{2,1,0:T(8,128)(2,1)} %bitcast.162), calls=%async_computation.7 | async-start | bytes 1048576 | tf_op jit(solution)/shard_map/all_to_all | solution.py:81
  195.7 7.5 %all-to-all-done.7 = bf16[128,16,128]{2,1,0:T(8,128)(2,1)} async-done(((bf16[128,16,128]{2,1,0:T(8,128)(2,1)}), bf16[128,16,128]{2,1,0:T(8,128)(2,1)}, u32[]{:S(2)}, u32[]{:S(2)}) %all-to-all-start.7) | async-done | bytes 524320 | tf_op jit(solution)/shard_map/all_to_all | solution.py:81
  205.4 2.8 %multiply_convert_fusion.5 = (bf16[128,16,128]{0,2,1:T(8,128)(2,1)S(1)}, bf16[128,16,128]{0,2,1:T(8,128)(2,1)S(1)}, bf16[128,16,128]{0,2,1:T(8,128)(2,1)S(1)}, bf16[128,16,128]{0,2,1:T(8,128)(2,1)S(1)}) fusion(bf16[128,16,128]{0,2,1:T(8,128)(2,1)S(1)} %copy.131, f32[256,16,128]{0,2,1:T(8,128)} %copy-done.4, f32[16,128]{1,0:T(8,128)S(1)} %broadcast_multiply_fusion, ...), kind=kLoop, calls=%fused_computation.134 | loop fusion | flops 6291456 | bytes 7348224 | tf_op jit(solution)/shard_map/convert.4
  214.1 17.5 %all_to_all.62 = bf16[128,16,128]{2,1,0:T(8,128)(2,1)S(1)} all-to-all(bf16[128,16,128]{2,1,0:T(8,128)(2,1)S(1)} %copy.137), channel_id=1, replica_groups=mesh['row'=32,'ch'=4] {'row','ch'}, dimensions={0} | all-to-all | bytes 1048576 | tf_op jit(solution)/shard_map/all_to_all | solution.py:61
  233.3 4.2 %all-to-all-start.11 = ((bf16[128,16,128]{2,1,0:T(8,128)(2,1)}), bf16[128,16,128]{2,1,0:T(8,128)(2,1)S(1)}, u32[]{:S(2)}, u32[]{:S(2)}) async-start(bf16[128,16,128]{2,1,0:T(8,128)(2,1)} %bitcast.53), calls=%async_computation.11 | async-start | bytes 1048576 | tf_op jit(solution)/shard_map/all_to_all | solution.py:88
  240.9 10.6 %all-to-all-done.11 = bf16[128,16,128]{2,1,0:T(8,128)(2,1)S(1)} async-done(((bf16[128,16,128]{2,1,0:T(8,128)(2,1)}), bf16[128,16,128]{2,1,0:T(8,128)(2,1)S(1)}, u32[]{:S(2)}, u32[]{:S(2)}) %all-to-all-start.11) | async-done | bytes 524320 | tf_op jit(solution)/shard_map/all_to_all | solution.py:88
  251.5 5.2 %all-to-all-start.10 = ((bf16[128,16,128]{2,1,0:T(8,128)(2,1)}), bf16[128,16,128]{2,1,0:T(8,128)(2,1)}, u32[]{:S(2)}, u32[]{:S(2)}) async-start(bf16[128,16,128]{2,1,0:T(8,128)(2,1)} %bitcast.50), calls=%async_computation.10 | async-start | bytes 1048576 | tf_op jit(solution)/shard_map/all_to_all | solution.py:81
  257.8 3.1 %fusion.86 = f32[16,128,128]{1,2,0:T(8,128)} fusion(f32[16,128,128]{1,2,0:T(8,128)} %get-tuple-element.46, f32[16,128,128]{1,2,0:T(8,128)} %copy-done.10, bf16[16,128,128]{1,2,0:T(8,128)(2,1)S(1)} %get-tuple-element.22, bf16[128,640]{0,1:T(8,128)(2,1)S(1)} %bitcast.176), kind=kOutput, calls=%fused_computation.145 | convolution fusion | flops 68681728 | bytes 3702784 | tf_op jit(solution)/shard_map/dot_general | solution.py:190
  263.0 7.3 %all-to-all-done.10 = bf16[128,16,128]{2,1,0:T(8,128)(2,1)} async-done(((bf16[128,16,128]{2,1,0:T(8,128)(2,1)}), bf16[128,16,128]{2,1,0:T(8,128)(2,1)}, u32[]{:S(2)}, u32[]{:S(2)}) %all-to-all-start.10) | async-done | bytes 524320 | tf_op jit(solution)/shard_map/all_to_all | solution.py:81
  (169 shorter events, 70.5 us)
Async XLA Ops:
  0.6 7.1 %copy-start.35 = (f32[2,2,128]{2,1,0:T(2,128)S(1)}, f32[2,2,128]{2,1,0:T(2,128)}, u32[]{:S(2)}) copy-start(f32[2,2,128]{2,1,0:T(2,128)} %param.15) | copy-start | bytes 6148
  0.6 7.1 %copy-start.36 = (f32[2,2,128]{2,1,0:T(2,128)S(1)}, f32[2,2,128]{2,1,0:T(2,128)}, u32[]{:S(2)}) copy-start(f32[2,2,128]{2,1,0:T(2,128)} %param.14) | copy-start | bytes 6148
  8.3 66.0 %copy-start.33 = (f32[128]{0:T(128)}, f32[128]{0:T(128)S(1)}, u32[]{:S(2)}) copy-start(f32[128]{0:T(128)S(1)} %get-tuple-element.56) | copy-start | bytes 1540
  8.3 66.4 %copy-start.29 = (f32[128]{0:T(128)}, f32[128]{0:T(128)S(1)}, u32[]{:S(2)}) copy-start(f32[128]{0:T(128)S(1)} %get-tuple-element.55) | copy-start | bytes 1540
  8.3 118.0 %copy-start.31 = (f32[128]{0:T(128)}, f32[128]{0:T(128)S(1)}, u32[]{:S(2)}) copy-start(f32[128]{0:T(128)S(1)} %get-tuple-element.54) | copy-start | bytes 1540
  12.0 25.3 %all-to-all-start = ((bf16[128,16,128]{2,1,0:T(8,128)(2,1)}), bf16[128,16,128]{2,1,0:T(8,128)(2,1)S(1)}, u32[]{:S(2)}, u32[]{:S(2)}) async-start(bf16[128,16,128]{2,1,0:T(8,128)(2,1)} %copy.102), calls=%async_computation | async-start | bytes 1048576 | tf_op jit(solution)/shard_map/all_to_all | solution.py:52
  37.3 18.1 %all-to-all-start.1 = ((bf16[128,16,128]{2,1,0:T(8,128)(2,1)}), bf16[128,16,128]{2,1,0:T(8,128)(2,1)S(1)}, u32[]{:S(2)}, u32[]{:S(2)}) async-start(bf16[128,16,128]{2,1,0:T(8,128)(2,1)} %copy.106), calls=%async_computation.1 | async-start | bytes 1048576 | tf_op jit(solution)/shard_map/all_to_all | solution.py:53
  41.8 14.7 %copy-start.17 = (bf16[1,32,16,4,128]{4,3,2,1,0:T(4,128)(2,1)}, bf16[1,32,16,4,128]{4,3,2,1,0:T(4,128)(2,1)S(1)}, u32[]{:S(2)}) copy-start(bf16[1,32,16,4,128]{4,3,2,1,0:T(4,128)(2,1)S(1)} %copy.103) | copy-start | bytes 1572868
  55.7 18.2 %copy-start.15 = (bf16[1,32,16,4,128]{4,3,2,1,0:T(4,128)(2,1)}, bf16[1,32,16,4,128]{4,3,2,1,0:T(4,128)(2,1)S(1)}, u32[]{:S(2)}) copy-start(bf16[1,32,16,4,128]{4,3,2,1,0:T(4,128)(2,1)S(1)} %copy.107) | copy-start | bytes 1572868
  56.2 18.1 %copy-start.23 = (bf16[2,128,128]{2,1,0:T(8,128)(2,1)S(1)}, bf16[2,128,128]{2,1,0:T(8,128)(2,1)}, u32[]{:S(2)}) copy-start(bf16[2,128,128]{2,1,0:T(8,128)(2,1)} %param.17) | copy-start | bytes 196612
  80.4 18.1 %all-to-all-start.3 = ((bf16[128,16,128]{2,1,0:T(8,128)(2,1)}), bf16[128,16,128]{2,1,0:T(8,128)(2,1)S(1)}, u32[]{:S(2)}, u32[]{:S(2)}) async-start(bf16[128,16,128]{2,1,0:T(8,128)(2,1)} %copy.114), calls=%async_computation.3 | async-start | bytes 1048576 | tf_op jit(solution)/shard_map/all_to_all | solution.py:52
  98.5 18.1 %all-to-all-start.4 = ((bf16[128,16,128]{2,1,0:T(8,128)(2,1)}), bf16[128,16,128]{2,1,0:T(8,128)(2,1)S(1)}, u32[]{:S(2)}, u32[]{:S(2)}) async-start(bf16[128,16,128]{2,1,0:T(8,128)(2,1)} %copy.117), calls=%async_computation.4 | async-start | bytes 1048576 | tf_op jit(solution)/shard_map/all_to_all | solution.py:53
  103.0 17.2 %copy-start.20 = (bf16[1,32,16,4,128]{4,3,2,1,0:T(4,128)(2,1)}, bf16[1,32,16,4,128]{4,3,2,1,0:T(4,128)(2,1)S(1)}, u32[]{:S(2)}) copy-start(bf16[1,32,16,4,128]{4,3,2,1,0:T(4,128)(2,1)S(1)} %copy.115) | copy-start | bytes 1572868
  119.0 6.3 %copy-start.14 = (bf16[16,128,128]{2,1,0:T(8,128)(2,1)S(1)}, bf16[16,128,128]{2,1,0:T(8,128)(2,1)}, u32[]{:S(2)}) copy-start(bf16[16,128,128]{2,1,0:T(8,128)(2,1)} %param.10) | copy-start | bytes 1572868
  121.1 18.1 %all-to-all-start.5 = ((bf16[128,16,128]{2,1,0:T(8,128)(2,1)}), bf16[128,16,128]{2,1,0:T(8,128)(2,1)S(1)}, u32[]{:S(2)}, u32[]{:S(2)}) async-start(bf16[128,16,128]{2,1,0:T(8,128)(2,1)} %bitcast.33), calls=%async_computation.5 | async-start | bytes 1048576 | tf_op jit(solution)/shard_map/all_to_all | solution.py:68
  141.5 18.9 %copy-start.21 = (bf16[1,32,16,4,128]{4,3,2,1,0:T(4,128)(2,1)S(1)}, bf16[1,32,16,4,128]{4,3,2,1,0:T(4,128)(2,1)}, u32[]{:S(2)}) copy-start(bf16[1,32,16,4,128]{4,3,2,1,0:T(4,128)(2,1)} %copy-done.20) | copy-start | bytes 1572868
  165.6 18.8 %all-to-all-start.8 = ((bf16[128,16,128]{2,1,0:T(8,128)(2,1)}), bf16[128,16,128]{2,1,0:T(8,128)(2,1)}, u32[]{:S(2)}, u32[]{:S(2)}) async-start(bf16[128,16,128]{2,1,0:T(8,128)(2,1)} %bitcast.165), calls=%async_computation.8 | async-start | bytes 1048576 | tf_op jit(solution)/shard_map/all_to_all | solution.py:88
  184.4 18.8 %all-to-all-start.7 = ((bf16[128,16,128]{2,1,0:T(8,128)(2,1)}), bf16[128,16,128]{2,1,0:T(8,128)(2,1)}, u32[]{:S(2)}, u32[]{:S(2)}) async-start(bf16[128,16,128]{2,1,0:T(8,128)(2,1)} %bitcast.162), calls=%async_computation.7 | async-start | bytes 1048576 | tf_op jit(solution)/shard_map/all_to_all | solution.py:81
  213.7 18.1 %copy-start.18 = (bf16[1,32,16,4,128]{4,3,2,1,0:T(4,128)(2,1)S(1)}, bf16[1,32,16,4,128]{4,3,2,1,0:T(4,128)(2,1)}, u32[]{:S(2)}) copy-start(bf16[1,32,16,4,128]{4,3,2,1,0:T(4,128)(2,1)} %copy-done.17) | copy-start | bytes 1572868
  232.3 5.3 %copy-start.16 = (bf16[1,32,16,4,128]{4,3,2,1,0:T(4,128)(2,1)S(1)}, bf16[1,32,16,4,128]{4,3,2,1,0:T(4,128)(2,1)}, u32[]{:S(2)}) copy-start(bf16[1,32,16,4,128]{4,3,2,1,0:T(4,128)(2,1)} %copy-done.15) | copy-start | bytes 1572868
  233.3 18.1 %all-to-all-start.11 = ((bf16[128,16,128]{2,1,0:T(8,128)(2,1)}), bf16[128,16,128]{2,1,0:T(8,128)(2,1)S(1)}, u32[]{:S(2)}, u32[]{:S(2)}) async-start(bf16[128,16,128]{2,1,0:T(8,128)(2,1)} %bitcast.53), calls=%async_computation.11 | async-start | bytes 1048576 | tf_op jit(solution)/shard_map/all_to_all | solution.py:88
  237.6 19.2 %copy-start.12 = (bf16[16,128,128]{1,2,0:T(8,128)(2,1)S(1)}, bf16[16,128,128]{1,2,0:T(8,128)(2,1)}, u32[]{:S(2)}) copy-start(bf16[16,128,128]{1,2,0:T(8,128)(2,1)} %get-tuple-element.23) | copy-start | bytes 1572868
  251.5 18.8 %all-to-all-start.10 = ((bf16[128,16,128]{2,1,0:T(8,128)(2,1)}), bf16[128,16,128]{2,1,0:T(8,128)(2,1)}, u32[]{:S(2)}, u32[]{:S(2)}) async-start(bf16[128,16,128]{2,1,0:T(8,128)(2,1)} %bitcast.50), calls=%async_computation.10 | async-start | bytes 1048576 | tf_op jit(solution)/shard_map/all_to_all | solution.py:81
  257.8 14.8 %copy-start.1 = (f32[256,16,128]{0,2,1:T(8,128)S(1)}, f32[256,16,128]{0,2,1:T(8,128)}, u32[]{:S(2)}) copy-start(f32[256,16,128]{0,2,1:T(8,128)} %copy-done) | copy-start | bytes 6291460
  (22 other events, 31.4 us)
where the time goes:
time: 280 us; the launch traced here: 279 us
  waiting for transfers between devices  97.5 us (35%)
  blocking collectives  52.5 us (19%)
  starting transfers between devices  48.3 us (17%)
  local copies, waits for them, and re-layouts  43.2 us (15%)
  matrix products  22.6 us (8%)
  other arithmetic  13.1 us (5%)
    all_to_all x2, blocking collectives, spread_cotangent(): lax.all_to_all(grad_tri, ('row', 'ch'), split_axis=0, concat_axis=0, tile...  35 us
    all_to_all x2, waiting for transfers between devices, spread_factors(): lax.all_to_all(right_factor, ('row', 'ch'), split_axis=0, concat_axis=0,...  27.3 us
    all_to_all x2, waiting for transfers between devices, spread_factors(): lax.all_to_all(left_factor, ('row', 'ch'), split_axis=0, concat_axis=0, t...  25.3 us
    all_to_all x2, waiting for transfers between devices, collect_grads(): lax.all_to_all(to_blocks(grad_right, row_count, col_count), ('row', 'ch')...  17.7 us
    all_to_all x1, blocking collectives, collect_product(): lax.all_to_all(to_blocks(product, row_count, col_count), ('row', 'ch'), s...  17.5 us
    all_to_all x2, starting transfers between devices, spread_factors(): lax.all_to_all(left_factor, ('row', 'ch'), split_axis=0, concat_axis=0, t...  15.7 us
    all_to_all x2, waiting for transfers between devices, collect_grads(): lax.all_to_all(to_blocks(grad_left, row_count, col_count), ('row', 'ch'),...  14.8 us
    all_to_all x1, waiting for transfers between devices, collect_product(): lax.all_to_all(to_blocks(product, row_count, col_count), ('row', 'ch'), s...  12.4 us
  transfers between devices with their start and end apart: 9, of which 9 were waited for; matrix products, arithmetic and copies ran while one was open for 9% of the time, Pallas kernels for 0%

commit v1 on v0

v1 whole, which is shorter than its diff:
```python
import jax
import jax.numpy as jnp
from jax import lax
from jax.sharding import PartitionSpec as P
from jax.experimental import pallas as pl
from jax.experimental.pallas import tpu as pltpu

EPS = 1e-05
MESH = pl.DeviceIdType.MESH
DEVICES = 128
UNITS = 12
SLABS = 8


def far_first(digit):
    return (digit + 2) - lax.div(digit, 2) * (2 * digit - 1)


def dot(first, second, first_dim=1, second_dim=0):
    return lax.dot_general(
        first,
        second,
        (((first_dim,), (second_dim,)), ((), ())),
        preferred_element_type=jnp.float32,
    )


def normalise(values):
    average = jnp.mean(values, axis=0, keepdims=True)
    centred = values - average
    spread = jnp.mean(centred * centred, axis=0, keepdims=True)
    inverse = lax.rsqrt(spread + EPS)
    return centred * inverse, inverse


def normalise_back(scaled_grad, unit, inverse):
    mean_grad = jnp.mean(scaled_grad, axis=0, keepdims=True)
    mean_prod = jnp.mean(scaled_grad * unit, axis=0, keepdims=True)
    return inverse * (scaled_grad - mean_grad - unit * mean_prod)


def twice(block):
    return jnp.concatenate([block, block], axis=1)


def kernel(
    pair_ref,
    gout_ref,
    valid_s,
    chain_s,
    valid_v,
    chain_v,
    table_ref,
    gain_ref,
    offset_ref,
    win_ref,
    wout_ref,
    final_ref,
    grad_ref,
    par,
    win_t,
    wout_t,
    mask,
    held,
    normed,
    lin,
    unit_t,
    inv_t,
    mixed_s,
    gtn,
    tnorm,
    gnorm,
    upper,
    stage_a,
    stage_b,
    snd,
    rcv,
    ssem,
    rsem,
):
    row, col = lax.axis_index("row"), lax.axis_index("ch")
    z, x = lax.div(row, 8), lax.rem(lax.div(row, 2), 4)
    y, core = lax.div(col, 2) * 2 + lax.rem(row, 2), lax.rem(col, 2)
    me = col * 32 + row

    def partner(t):
        z2 = lax.rem(z + far_first(lax.rem(lax.div(t, 16), 4)), 4)
        x2 = lax.rem(x + far_first(lax.rem(lax.div(t, 4), 4)), 4)
        y2 = lax.rem(y + far_first(lax.rem(t, 4)), 4)
        c2 = lax.rem(core + 1 - lax.div(t, 64), 2)
        return z2 * 8 + x2 * 2 + lax.rem(y2, 2), lax.div(y2, 2) * 2 + c2

    barrier = pltpu.get_barrier_semaphore()

    def greet(t, carry):
        pl.semaphore_signal(barrier, inc=1, device_id=partner(t), device_id_type=MESH)
        return carry

    lax.fori_loop(0, DEVICES - 1, greet, 0)

    def send(u):
        rcv[u, me] = snd[u, me]

        def step(t, carry):
            r2, h2 = partner(t)
            pltpu.make_async_remote_copy(
                src_ref=snd.at[u, h2 * 32 + r2],
                dst_ref=rcv.at[u, me],
                send_sem=ssem.at[u],
                recv_sem=rsem.at[u],
                device_id=(r2, h2),
                device_id_type=MESH,
            ).start()
            return carry

        lax.fori_loop(0, DEVICES - 1, step, 0)

    def whole(u):
        return pltpu.make_async_remote_copy(
            src_ref=snd.at[u, pl.ds(0, DEVICES - 1)],
            dst_ref=rcv.at[u, pl.ds(0, DEVICES - 1)],
            send_sem=ssem.at[u],
            recv_sem=rsem.at[u],
            device_id=(row, col),
            device_id_type=MESH,
        )

    def each_slab(body):
        def step(s, carry):
            body(s)
            return carry

        lax.fori_loop(0, SLABS, step, 0)

    def put(stage, s, value):
        stage[pl.ds(2 * s, 128, stride=16), :] = value[:, :128]
        stage[pl.ds(2 * s + 1, 128, stride=16), :] = value[:, 128:]

    def get(stage, s):
        return jnp.concatenate(
            [stage[pl.ds(2 * s, 128, stride=16), :], stage[pl.ds(2 * s + 1, 128, stride=16), :]],
            axis=1,
        )

    def flush(stage, u):
        def step(q, carry):
            part = stage[pl.ds(pl.multiple_of(q * 256, 256), 256), :]
            snd[u, pl.ds(q * 16, 16)] = part.astype(jnp.bfloat16).reshape(16, 16, 128)
            return carry

        lax.fori_loop(0, 8, step, 0)
        send(u)

    def fetch(u, stage):
        whole(u).wait_recv()

        def step(q, carry):
            part = rcv[u, pl.ds(q * 16, 16)].reshape(256, 128)
            stage[pl.ds(pl.multiple_of(q * 256, 256), 256), :] = part.astype(jnp.float32)
            return carry

        lax.fori_loop(0, 8, step, 0)

    def gain(layer, which):
        return twice(par[2 + 2 * layer + which])

    def offset(layer, which):
        return twice(par[6 + 2 * layer + which])

    def column(row_values):
        return jnp.transpose(jnp.broadcast_to(row_values, (128, 128)))

    def prepare(layer):
        for which in range(2):
            k = 2 * layer + which
            par[2 + k] = column(gain_ref[k : k + 1, :])
            par[6 + k] = column(offset_ref[k : k + 1, :])
        for part in range(5):
            block = win_ref[layer, :, part * 128 : (part + 1) * 128].astype(jnp.float32)
            win_t[layer, part * 128 : (part + 1) * 128, :] = jnp.transpose(block).astype(
                jnp.bfloat16
            )
        wout_t[layer] = jnp.transpose(wout_ref[layer].astype(jnp.float32)).astype(jnp.bfloat16)

    def matrix(u, first=0, count=32):
        return jnp.concatenate(
            [
                rcv[u, 32 * h + first : 32 * h + first + count].reshape(16 * count, 128)
                for h in range(4)
            ],
            axis=1,
        )

    def multiply(u_first, flip_first, u_second, flip_second, u_out):
        second = matrix(u_second)
        for m in range(2):
            if flip_first:
                first = jnp.concatenate(
                    [
                        rcv[u_first, 32 * h : 32 * h + 32].reshape(512, 128)
                        for h in (2 * m, 2 * m + 1)
                    ],
                    axis=1,
                )
            else:
                first = matrix(u_first, 16 * m, 16)
            result = dot(first, second, 0 if flip_first else 1, 1 if flip_second else 0)
            result = result.astype(jnp.bfloat16)
            for h in range(4):
                snd[u_out, 32 * h + 16 * m : 32 * h + 16 * m + 16] = result[
                    :, 128 * h : 128 * h + 128
                ].reshape(16, 16, 128)
        send(u_out)

    def factor(layer, s, part, stage):
        both = dot(win_t[layer, 256 * part : 256 * part + 256, :], normed[s])
        squash = jax.nn.sigmoid(both[:128])
        value = both[128:]
        lin[layer, s, 256 * part : 256 * part + 128, :] = squash
        lin[layer, s, 256 * part + 128 : 256 * part + 256, :] = value
        put(stage, s, mask[s, 0:1, :] * (squash * value))

    def input_norm(layer, s, values):
        unit, _ = normalise(values)
        normed[s] = (unit * gain(layer, 0) + offset(layer, 0)).astype(jnp.bfloat16)

    def open_gate(layer, s):
        lin[layer, s, 512:640, :] = jax.nn.sigmoid(dot(win_t[layer, 512:640, :], normed[s]))

    def product_norm(layer, s, stage):
        unit, inverse = normalise(get(stage, s))
        return unit, inverse, (unit * gain(layer, 1) + offset(layer, 1)).astype(jnp.bfloat16)

    def mixed_back(layer, s, upstream):
        grad_mixed = (upstream * lin[layer, s, 512:640, :]).astype(jnp.bfloat16)
        return dot(wout_ref[layer], grad_mixed)

    def gate_back(layer, s, upstream, mixed):
        gate = lin[layer, s, 512:640, :]
        back = (upstream * mixed * gate * (1.0 - gate)).astype(jnp.bfloat16)
        gnorm[s] = dot(win_ref[layer, :, 512:640], back)

    def factor_back(layer, s, part, stage):
        squash = lin[layer, s, 256 * part : 256 * part + 128, :]
        value = lin[layer, s, 256 * part + 128 : 256 * part + 256, :]
        cotangent = mask[s, 0:1, :] * get(stage, s)
        last = cotangent * squash
        first = last * value * (1.0 - squash)
        both = jnp.concatenate([first.astype(jnp.bfloat16), last.astype(jnp.bfloat16)], axis=0)
        return gnorm[s] + dot(win_ref[layer, :, 256 * part : 256 * part + 256], both)

    def input_back(layer, s, grad_normed):
        unit, inverse = normalise(held[layer, s].astype(jnp.float32))
        back = normalise_back(grad_normed * gain(layer, 0), unit, inverse)
        return (upper[s].astype(jnp.float32) + back).astype(jnp.bfloat16)

    par[0] = column(table_ref[0:1, :])
    par[1] = column(table_ref[1:2, :])
    prepare(0)
    valid_cols = valid_v[pl.ds(col, 1), :].astype(jnp.float32)
    chain_cols = chain_v[pl.ds(col, 1), :]

    def enter(s):
        parts, masks = [], []
        for k in range(2):
            at = row * 16 + 2 * s + k
            masks.append(valid_s[at].astype(jnp.float32) * valid_cols)
            same = (chain_cols == chain_s[at]).astype(jnp.float32)
            block = jnp.transpose(pair_ref[2 * s + k].astype(jnp.float32))
            parts.append(block + same * par[1] + (1.0 - same) * par[0])
        mask[s] = jnp.broadcast_to(jnp.concatenate(masks, axis=1), (8, 256))
        entry = jnp.concatenate(parts, axis=1).astype(jnp.bfloat16)
        held[0, s] = entry
        input_norm(0, s, entry.astype(jnp.float32))
        factor(0, s, 0, stage_a)

    each_slab(enter)
    pl.semaphore_wait(barrier, DEVICES - 1)
    flush(stage_a, 0)
    each_slab(lambda s: factor(0, s, 1, stage_b))
    flush(stage_b, 1)

    def rest_of_entry(s):
        open_gate(0, s)
        parts = [jnp.transpose(gout_ref[2 * s + k].astype(jnp.float32)) for k in range(2)]
        upper[s] = jnp.concatenate(parts, axis=1).astype(jnp.bfloat16)

    each_slab(rest_of_entry)
    prepare(1)
    whole(0).wait_recv()
    whole(1).wait_recv()
    multiply(0, False, 1, True, 2)

    fetch(2, stage_a)

    def middle(s):
        unit, inverse, scaled = product_norm(0, s, stage_a)
        unit_t[s] = unit
        inv_t[s] = jnp.broadcast_to(inverse, (8, 256))
        mixed = dot(wout_t[0], scaled)
        mixed_s[s] = mixed
        value = held[0, s].astype(jnp.float32) + lin[0, s, 512:640, :] * mixed
        value = value.astype(jnp.bfloat16)
        held[1, s] = value
        input_norm(1, s, value.astype(jnp.float32))
        factor(1, s, 0, stage_b)

    each_slab(middle)
    flush(stage_b, 3)
    each_slab(lambda s: factor(1, s, 1, stage_a))
    flush(stage_a, 4)

    def rest_of_middle(s):
        open_gate(1, s)
        gtn[s] = mixed_back(1, s, upper[s].astype(jnp.float32))

    each_slab(rest_of_middle)
    whole(3).wait_recv()
    whole(4).wait_recv()
    multiply(3, True, 4, False, 5)

    fetch(5, stage_a)

    def turn(s):
        unit, inverse, scaled = product_norm(1, s, stage_a)
        tnorm[s] = scaled
        put(stage_b, s, normalise_back(gtn[s] * gain(1, 1), unit, inverse))

    each_slab(turn)
    flush(stage_b, 6)

    def finish(s):
        mixed = dot(wout_t[1], tnorm[s])
        value = held[1, s].astype(jnp.float32) + lin[1, s, 512:640, :] * mixed
        for k in range(2):
            final_ref[2 * s + k] = jnp.transpose(value[:, 128 * k : 128 * k + 128]).astype(
                jnp.bfloat16
            )
        gate_back(1, s, upper[s].astype(jnp.float32), mixed)

    each_slab(finish)
    whole(6).wait_recv()
    multiply(4, False, 6, True, 7)
    multiply(3, False, 6, False, 8)
    fetch(7, stage_a)

    def left_back(layer, s):
        gnorm[s] = factor_back(layer, s, 0, stage_a)

    each_slab(lambda s: left_back(1, s))
    fetch(8, stage_b)

    def lower(s):
        value = input_back(1, s, factor_back(1, s, 1, stage_b))
        upper[s] = value
        grad_tnorm = mixed_back(0, s, value.astype(jnp.float32))
        put(stage_a, s, normalise_back(grad_tnorm * gain(0, 1), unit_t[s], inv_t[s, 0:1, :]))

    each_slab(lower)
    flush(stage_a, 9)
    each_slab(lambda s: gate_back(0, s, upper[s].astype(jnp.float32), mixed_s[s]))
    whole(9).wait_recv()
    multiply(9, False, 1, False, 10)
    multiply(9, True, 0, False, 11)
    fetch(10, stage_a)
    each_slab(lambda s: left_back(0, s))
    fetch(11, stage_b)

    def leave(s):
        value = input_back(0, s, factor_back(0, s, 1, stage_b)).astype(jnp.float32)
        for k in range(2):
            grad_ref[2 * s + k] = jnp.transpose(value[:, 128 * k : 128 * k + 128]).astype(
                jnp.bfloat16
            )

    each_slab(leave)
    for u in range(UNITS):
        whole(u).wait_send()


def local(
    pair_in,
    grad_out,
    token_valid,
    chain_ids,
    chain_table,
    norm_gain,
    norm_offset,
    proj_in,
    proj_out,
):
    vmem = pl.BlockSpec(memory_space=pltpu.VMEM)
    smem = pl.BlockSpec(memory_space=pltpu.SMEM)
    bf16, f32 = jnp.bfloat16, jnp.float32
    scratch = [
        pltpu.VMEM((10, 128, 128), f32),
        pltpu.VMEM((2, 640, 128), bf16),
        pltpu.VMEM((2, 128, 128), bf16),
        pltpu.VMEM((SLABS, 8, 256), f32),
        pltpu.VMEM((2, SLABS, 128, 256), bf16),
        pltpu.VMEM((SLABS, 128, 256), bf16),
        pltpu.VMEM((2, SLABS, 640, 256), f32),
        pltpu.VMEM((SLABS, 128, 256), f32),
        pltpu.VMEM((SLABS, 8, 256), f32),
        pltpu.VMEM((SLABS, 128, 256), f32),
        pltpu.VMEM((SLABS, 128, 256), f32),
        pltpu.VMEM((SLABS, 128, 256), bf16),
        pltpu.VMEM((SLABS, 128, 256), f32),
        pltpu.VMEM((SLABS, 128, 256), bf16),
        pltpu.VMEM((2048, 128), f32),
        pltpu.VMEM((2048, 128), f32),
        pltpu.VMEM((UNITS, DEVICES, 16, 128), bf16),
        pltpu.VMEM((UNITS, DEVICES, 16, 128), bf16),
        pltpu.SemaphoreType.DMA((UNITS,)),
        pltpu.SemaphoreType.DMA((UNITS,)),
    ]
    shape = jax.ShapeDtypeStruct(pair_in.shape, bf16)
    return pl.pallas_call(
        kernel,
        out_shape=(shape, shape),
        in_specs=[vmem, vmem, smem, smem] + [vmem] * 7,
        out_specs=(vmem, vmem),
        scratch_shapes=scratch,
        compiler_params=pltpu.CompilerParams(
            collective_id=0, has_side_effects=True, vmem_limit_bytes=56 * 1024 * 1024
        ),
    )(
        pair_in,
        grad_out,
        token_valid,
        chain_ids,
        token_valid.reshape(4, 128),
        chain_ids.reshape(4, 128),
        chain_table,
        norm_gain.reshape(4, 128),
        norm_offset.reshape(4, 128),
        proj_in,
        proj_out,
    )


def solution(mesh):
    in_specs = (P("row", "ch", None), P("row", "ch", None), P(), P(), P(), P(), P(), P(), P())
    out_specs = (P("row", "ch", None), P("row", "ch", None))
    return jax.shard_map(local, mesh=mesh, in_specs=in_specs, out_specs=out_specs, check_vma=False)
```

time: 280 us -> 133 us (0.47)
  Pallas kernels: 0 us -> 130 us
  waiting for transfers between devices: 97.5 us -> 0 us
  blocking collectives: 52.5 us -> 0 us
  starting transfers between devices: 48.3 us -> 0 us
  local copies, waits for them, and re-layouts: 43.2 us -> 2.74 us
  matrix products: 22.6 us -> 0 us
  other arithmetic: 13.1 us -> 0 us
    pallas_call x0 -> x1, Pallas kernels: none -> 130 us  [local(): pl.pallas_call(kernel, out_shape=(shape, shape), in_specs=[vmem, vmem, sm...]
    all_to_all x9 -> x0, waiting for transfers between devices: 97.5 us -> none  [the longest x2 27.3 us: spread_factors(): lax.all_to_all(right_factor, ('row', 'ch'), split_axis=0, concat_axis=0,...]
    all_to_all x3 -> x0, blocking collectives: 52.5 us -> none  [the longest x2 35 us: spread_cotangent(): lax.all_to_all(grad_tri, ('row', 'ch'), split_axis=0, concat_axis=0, tile...]
    all_to_all x9 -> x0, starting transfers between devices: 48.3 us -> none  [the longest x2 15.7 us: spread_factors(): lax.all_to_all(left_factor, ('row', 'ch'), split_axis=0, concat_axis=0, t...]
    dot_general x22 -> x0, matrix products: 22.6 us -> none  [the longest x6 7.18 us: batched_dot(): lax.dot_general(first, second, (((first_dim,), (second_dim,)), ((0,), (0,...]
    reshape x12 -> x0, local copies, waits for them, and re-layouts: 12.8 us -> none  [the longest x10 12.3 us: to_blocks(): channels.reshape(per_dev, row_count, total_rows // row_count, col_count,...]
    unnamed x79 -> x4, local copies, waits for them, and re-layouts: 11 us -> 2.74 us
    all_to_all x4 -> x0, local copies, waits for them, and re-layouts: 8.15 us -> none  [the longest x2 4.46 us: collect_grads(): lax.all_to_all(to_blocks(grad_left, row_count, col_count), ('row', 'ch'),...]
  transfers between devices with their start and end apart: 9 -> 0, of which waited for: 9 -> 0; matrix products, arithmetic and copies ran while one was open for 9% -> 0% of each run, Pallas kernels for 0% -> 0%
where the time goes in v1:
time: 133 us
  Pallas kernels  130 us (98%)
  local copies, waits for them, and re-layouts  2.74 us (2%)
    pallas_call x1, Pallas kernels, local(): pl.pallas_call(kernel, out_shape=(shape, shape), in_specs=[vmem, vmem, sm...  130 us
    unnamed x4, local copies, waits for them, and re-layouts  2.74 us

profile of v1, /device:TPU:1, one launch (start us, length us, event | category | flops | bytes accessed | tf_op | source)
XLA Modules:
  0.0 133.3 jit_solution(12232736126500521204)
XLA Ops:
  0.6 129.9 %shard_map.104 = (bf16[16,128,128]{2,1,0:T(8,128)(2,1)}, bf16[16,128,128]{2,1,0:T(8,128)(2,1)}) custom-call(bf16[16,128,128]{2,1,0:T(8,128)(2,1)} %pair_ref.1, bf16[16,128,128]{2,1,0:T(8,128)(2,1)} %gout_ref.1, s32[512]{0:T(512)} %valid_s.1, s32[512]{0:T(512)} %chain_s.1, s32[4,128]{1,0:T(4,128)} %bitcast.4, s32[4,128]{1,0:T(4,128)} %bitcast.5, ...), custom_call_target="tpu_custom_call" | custom-call | tf_op jit(solution)/shard_map/pallas_call | solution.py:418
  130.6 0.0 copy-start
  130.6 1.9 %copy.13 = bf16[16,128,128]{2,1,0:T(8,128)(2,1)} copy(bf16[16,128,128]{2,1,0:T(8,128)(2,1)} %get-tuple-element.4) | data formatting | bytes 1048576
  132.5 0.0 copy-done
  132.5 0.8 copy.14
Async XLA Ops:
  130.6 2.0 %copy-start = (bf16[16,128,128]{2,1,0:T(8,128)(2,1)S(1)}, bf16[16,128,128]{2,1,0:T(8,128)(2,1)}, u32[]{:S(2)}) copy-start(bf16[16,128,128]{2,1,0:T(8,128)(2,1)} %get-tuple-element.5) | copy-start | bytes 1572868

commit v2 on v1

--- a/solution.py
+++ b/solution.py
@@ -130,7 +130,7 @@
             body(s)
             return carry
 
-        lax.fori_loop(0, SLABS, step, 0)
+        lax.fori_loop(0, SLABS, step, 0, unroll=4)
 
     def put(stage, s, value):
         stage[pl.ds(2 * s, 128, stride=16), :] = value[:, :128]
@@ -148,7 +148,7 @@
             snd[u, pl.ds(q * 16, 16)] = part.astype(jnp.bfloat16).reshape(16, 16, 128)
             return carry
 
-        lax.fori_loop(0, 8, step, 0)
+        lax.fori_loop(0, 8, step, 0, unroll=4)
         send(u)
 
     def fetch(u, stage):
@@ -159,7 +159,7 @@
             stage[pl.ds(pl.multiple_of(q * 256, 256), 256), :] = part.astype(jnp.float32)
             return carry
 
-        lax.fori_loop(0, 8, step, 0)
+        lax.fori_loop(0, 8, step, 0, unroll=4)
 
     def gain(layer, which):
         return twice(par[2 + 2 * layer + which])

time: 133 us -> 126 us (0.947)
  Pallas kernels: 130 us -> 122 us
    pallas_call x1, Pallas kernels: 130 us -> 122 us  [local(): pl.pallas_call(kernel, out_shape=(shape, shape), in_specs=[vmem, vmem, sm...]
where the time goes in v2:
time: 126 us; the launch traced here: 125 us
  Pallas kernels  122 us (97%)
  local copies, waits for them, and re-layouts  2.74 us (2%)
    pallas_call x1, Pallas kernels, local(): pl.pallas_call(kernel, out_shape=(shape, shape), in_specs=[vmem, vmem, sm...  122 us
    unnamed x4, local copies, waits for them, and re-layouts  2.74 us

profile of v2, /device:TPU:1, one launch (start us, length us, event | category | flops | bytes accessed | tf_op | source)
XLA Modules:
  0.0 125.3 jit_solution(5513258937336017767)
XLA Ops:
  0.6 122.0 %shard_map.104 = (bf16[16,128,128]{2,1,0:T(8,128)(2,1)}, bf16[16,128,128]{2,1,0:T(8,128)(2,1)}) custom-call(bf16[16,128,128]{2,1,0:T(8,128)(2,1)} %pair_ref.1, bf16[16,128,128]{2,1,0:T(8,128)(2,1)} %gout_ref.1, s32[512]{0:T(512)} %valid_s.1, s32[512]{0:T(512)} %chain_s.1, s32[4,128]{1,0:T(4,128)} %bitcast.4, s32[4,128]{1,0:T(4,128)} %bitcast.5, ...), custom_call_target="tpu_custom_call" | custom-call | tf_op jit(solution)/shard_map/pallas_call | solution.py:418
  122.6 0.0 copy-start
  122.6 1.9 %copy.13 = bf16[16,128,128]{2,1,0:T(8,128)(2,1)} copy(bf16[16,128,128]{2,1,0:T(8,128)(2,1)} %get-tuple-element.4) | data formatting | bytes 1048576
  124.6 0.0 copy-done
  124.6 0.8 copy.14
Async XLA Ops:
  122.6 2.0 %copy-start = (bf16[16,128,128]{2,1,0:T(8,128)(2,1)S(1)}, bf16[16,128,128]{2,1,0:T(8,128)(2,1)}, u32[]{:S(2)}) copy-start(bf16[16,128,128]{2,1,0:T(8,128)(2,1)} %get-tuple-element.5) | copy-start | bytes 1572868

commit v3 on v2

--- a/solution.py
+++ b/solution.py
@@ -9,6 +9,7 @@
 MESH = pl.DeviceIdType.MESH
 DEVICES = 128
 UNITS = 12
+FAR_FIRST = (2, 3, 1, 0)
 SLABS = 8
 
 
@@ -83,27 +84,34 @@
     y, core = lax.div(col, 2) * 2 + lax.rem(row, 2), lax.rem(col, 2)
     me = col * 32 + row
 
-    def partner(t):
-        z2 = lax.rem(z + far_first(lax.rem(lax.div(t, 16), 4)), 4)
-        x2 = lax.rem(x + far_first(lax.rem(lax.div(t, 4), 4)), 4)
-        y2 = lax.rem(y + far_first(lax.rem(t, 4)), 4)
-        c2 = lax.rem(core + 1 - lax.div(t, 64), 2)
-        return z2 * 8 + x2 * 2 + lax.rem(y2, 2), lax.div(y2, 2) * 2 + c2
+    xs = [lax.rem(x + q, 4) * 2 for q in FAR_FIRST]
+    ys = [lax.rem(y + q, 4) for q in FAR_FIRST]
+    ys = [(lax.rem(value, 2), lax.div(value, 2) * 2) for value in ys]
+    spots = [(x_part + low, high) for x_part in xs for low, high in ys]
+
+    def each_partner(act):
+        def step(t, carry):
+            r2 = lax.rem(z + far_first(lax.rem(t, 4)), 4) * 8
+            h2 = lax.rem(core + 1 - lax.div(t, 4), 2)
+            for r_part, h_part in spots:
+                act(r2 + r_part, h2 + h_part)
+            return carry
+
+        lax.fori_loop(0, 7, step, 0)
+        for r_part, h_part in spots[:-1]:
+            act(z * 8 + r_part, core + h_part)
 
     barrier = pltpu.get_barrier_semaphore()
-
-    def greet(t, carry):
-        pl.semaphore_signal(barrier, inc=1, device_id=partner(t), device_id_type=MESH)
-        return carry
-
-    lax.fori_loop(0, DEVICES - 1, greet, 0)
+    each_partner(
+        lambda r2, h2: pl.semaphore_signal(
+            barrier, inc=1, device_id=(r2, h2), device_id_type=MESH
+        )
+    )
 
     def send(u):
         rcv[u, me] = snd[u, me]
-
-        def step(t, carry):
-            r2, h2 = partner(t)
-            pltpu.make_async_remote_copy(
+        each_partner(
+            lambda r2, h2: pltpu.make_async_remote_copy(
                 src_ref=snd.at[u, h2 * 32 + r2],
                 dst_ref=rcv.at[u, me],
                 send_sem=ssem.at[u],
@@ -111,9 +119,7 @@
                 device_id=(r2, h2),
                 device_id_type=MESH,
             ).start()
-            return carry
-
-        lax.fori_loop(0, DEVICES - 1, step, 0)
+        )
 
     def whole(u):
         return pltpu.make_async_remote_copy(
@@ -130,7 +136,7 @@
             body(s)
             return carry
 
-        lax.fori_loop(0, SLABS, step, 0, unroll=4)
+        lax.fori_loop(0, SLABS, step, 0, unroll=8)
 
     def put(stage, s, value):
         stage[pl.ds(2 * s, 128, stride=16), :] = value[:, :128]
@@ -148,7 +154,7 @@
             snd[u, pl.ds(q * 16, 16)] = part.astype(jnp.bfloat16).reshape(16, 16, 128)
             return carry
 
-        lax.fori_loop(0, 8, step, 0, unroll=4)
+        lax.fori_loop(0, 8, step, 0, unroll=8)
         send(u)
 
     def fetch(u, stage):
@@ -159,7 +165,7 @@
             stage[pl.ds(pl.multiple_of(q * 256, 256), 256), :] = part.astype(jnp.float32)
             return carry
 
-        lax.fori_loop(0, 8, step, 0, unroll=4)
+        lax.fori_loop(0, 8, step, 0, unroll=8)
 
     def gain(layer, which):
         return twice(par[2 + 2 * layer + which])

time: 126 us -> 115 us (0.913)
  Pallas kernels: 122 us -> 111 us
    pallas_call x1, Pallas kernels: 122 us -> 111 us  [local(): pl.pallas_call(kernel, out_shape=(shape, shape), in_specs=[vmem, vmem, sm...]
where the time goes in v3:
time: 115 us; the launch traced here: 114 us
  Pallas kernels  111 us (97%)
  local copies, waits for them, and re-layouts  2.74 us (2%)
    pallas_call x1, Pallas kernels, local(): pl.pallas_call(kernel, out_shape=(shape, shape), in_specs=[vmem, vmem, sm...  111 us
    unnamed x4, local copies, waits for them, and re-layouts  2.74 us

profile of v3, /device:TPU:1, one launch (start us, length us, event | category | flops | bytes accessed | tf_op | source)
XLA Modules:
  0.0 114.4 jit_solution(12372234709159059287)
XLA Ops:
  0.6 111.0 %shard_map.104 = (bf16[16,128,128]{2,1,0:T(8,128)(2,1)}, bf16[16,128,128]{2,1,0:T(8,128)(2,1)}) custom-call(bf16[16,128,128]{2,1,0:T(8,128)(2,1)} %pair_ref.1, bf16[16,128,128]{2,1,0:T(8,128)(2,1)} %gout_ref.1, s32[512]{0:T(512)} %valid_s.1, s32[512]{0:T(512)} %chain_s.1, s32[4,128]{1,0:T(4,128)} %bitcast.4, s32[4,128]{1,0:T(4,128)} %bitcast.5, ...), custom_call_target="tpu_custom_call" | custom-call | tf_op jit(solution)/shard_map/pallas_call | solution.py:424
  111.6 0.0 copy-start
  111.7 1.9 %copy.13 = bf16[16,128,128]{2,1,0:T(8,128)(2,1)} copy(bf16[16,128,128]{2,1,0:T(8,128)(2,1)} %get-tuple-element.4) | data formatting | bytes 1048576
  113.6 0.0 copy-done
  113.6 0.8 copy.14
Async XLA Ops:
  111.6 2.0 %copy-start = (bf16[16,128,128]{2,1,0:T(8,128)(2,1)S(1)}, bf16[16,128,128]{2,1,0:T(8,128)(2,1)}, u32[]{:S(2)}) copy-start(bf16[16,128,128]{2,1,0:T(8,128)(2,1)} %get-tuple-element.5) | copy-start | bytes 1572868

commit v4 on v3

--- a/solution.py
+++ b/solution.py
@@ -89,47 +89,70 @@
     ys = [(lax.rem(value, 2), lax.div(value, 2) * 2) for value in ys]
     spots = [(x_part + low, high) for x_part in xs for low, high in ys]
 
-    def each_partner(act):
+    def by_core(t):
+        plane = lax.rem(z + far_first(lax.rem(t, 4)), 4)
+        return plane, lax.rem(core + 1 - lax.div(t, 4), 2), lax.div(t, 4)
+
+    def by_half(t):
+        plane = lax.rem(z + far_first(2 * lax.div(t, 4) + lax.rem(t, 2)), 4)
+        return plane, lax.rem(core + 1 - lax.rem(lax.div(t, 2), 2), 2), lax.div(t, 4)
+
+    def to_each(act, order, first, count, with_self):
         def step(t, carry):
-            r2 = lax.rem(z + far_first(lax.rem(t, 4)), 4) * 8
-            h2 = lax.rem(core + 1 - lax.div(t, 4), 2)
+            plane, core2, part = order(t)
             for r_part, h_part in spots:
-                act(r2 + r_part, h2 + h_part)
+                act(plane * 8 + r_part, core2 + h_part, part)
             return carry
 
-        lax.fori_loop(0, 7, step, 0)
-        for r_part, h_part in spots[:-1]:
-            act(z * 8 + r_part, core + h_part)
+        lax.fori_loop(first, first + count - (1 if with_self else 0), step, 0)
+        if with_self:
+            part = order(jnp.int32(first + count - 1))[2]
+            for r_part, h_part in spots[:-1]:
+                act(z * 8 + r_part, core + h_part, part)
 
     barrier = pltpu.get_barrier_semaphore()
-    each_partner(
-        lambda r2, h2: pl.semaphore_signal(
+    to_each(
+        lambda r2, h2, part: pl.semaphore_signal(
             barrier, inc=1, device_id=(r2, h2), device_id_type=MESH
-        )
+        ),
+        by_core,
+        0,
+        8,
+        True,
     )
 
-    def send(u):
-        rcv[u, me] = snd[u, me]
-        each_partner(
-            lambda r2, h2: pltpu.make_async_remote_copy(
+    def copy_to(u, split):
+        def act(r2, h2, part):
+            pltpu.make_async_remote_copy(
                 src_ref=snd.at[u, h2 * 32 + r2],
                 dst_ref=rcv.at[u, me],
                 send_sem=ssem.at[u],
-                recv_sem=rsem.at[u],
+                recv_sem=rsem.at[u, part if split else 0],
                 device_id=(r2, h2),
                 device_id_type=MESH,
             ).start()
-        )
-
-    def whole(u):
+
+        return act
+
+    def keep(u):
+        rcv[u, me] = snd[u, me]
+
+    def send(u, split=False, order=by_core):
+        keep(u)
+        to_each(copy_to(u, split), order, 0, 8, True)
+
+    def whole(u, part=0, count=DEVICES - 1):
         return pltpu.make_async_remote_copy(
-            src_ref=snd.at[u, pl.ds(0, DEVICES - 1)],
-            dst_ref=rcv.at[u, pl.ds(0, DEVICES - 1)],
+            src_ref=snd.at[u, pl.ds(0, count)],
+            dst_ref=rcv.at[u, pl.ds(0, count)],
             send_sem=ssem.at[u],
-            recv_sem=rsem.at[u],
+            recv_sem=rsem.at[u, part],
             device_id=(row, col),
             device_id_type=MESH,
         )
+
+    def wait_part(u, part):
+        whole(u, part, 64 - part).wait_recv()
 
     def each_slab(body):
         def step(s, carry):
@@ -148,14 +171,14 @@
             axis=1,
         )
 
-    def flush(stage, u):
+    def flush(stage, u, split=False, order=by_core):
         def step(q, carry):
             part = stage[pl.ds(pl.multiple_of(q * 256, 256), 256), :]
             snd[u, pl.ds(q * 16, 16)] = part.astype(jnp.bfloat16).reshape(16, 16, 128)
             return carry
 
         lax.fori_loop(0, 8, step, 0, unroll=8)
-        send(u)
+        send(u, split, order)
 
     def fetch(u, stage):
         whole(u).wait_recv()
@@ -197,26 +220,91 @@
             axis=1,
         )
 
-    def multiply(u_first, flip_first, u_second, flip_second, u_out):
+    def column_of(u, h):
+        return rcv[u, pl.ds(32 * h, 32)].reshape(512, 128)
+
+    def plane_rows(u, plane):
+        return jnp.concatenate(
+            [rcv[u, pl.ds(32 * h + 8 * plane, 8)].reshape(128, 128) for h in range(4)], axis=1
+        )
+
+    def store_rows(u, plane, result):
+        result = result.astype(jnp.bfloat16)
+        for h in range(4):
+            part = result[:, 128 * h : 128 * h + 128]
+            snd[u, pl.ds(32 * h + 8 * plane, 8)] = part.reshape(8, 16, 128)
+
+    def multiply(u_first, u_second, flip_second, u_out):
         second = matrix(u_second)
         for m in range(2):
-            if flip_first:
-                first = jnp.concatenate(
-                    [
-                        rcv[u_first, 32 * h : 32 * h + 32].reshape(512, 128)
-                        for h in (2 * m, 2 * m + 1)
-                    ],
-                    axis=1,
-                )
-            else:
-                first = matrix(u_first, 16 * m, 16)
-            result = dot(first, second, 0 if flip_first else 1, 1 if flip_second else 0)
+            result = dot(matrix(u_first, 16 * m, 16), second, 1, 1 if flip_second else 0)
             result = result.astype(jnp.bfloat16)
             for h in range(4):
                 snd[u_out, 32 * h + 16 * m : 32 * h + 16 * m + 16] = result[
                     :, 128 * h : 128 * h + 128
                 ].reshape(16, 16, 128)
         send(u_out)
+
+    def rows_by_half(u_first, u_second, u_out):
+        second = matrix(u_second)
+        for part in range(2):
+            wait_part(u_first, part)
+            planes = [lax.rem(z + 4 - FAR_FIRST[2 * part + k], 4) for k in range(2)]
+            both = jnp.concatenate([plane_rows(u_first, plane) for plane in planes], axis=0)
+            result = dot(both, second, 1, 1)
+            for k in range(2):
+                store_rows(u_out, planes[k], result[128 * k : 128 * k + 128])
+
+            def order(t):
+                step = 3 - 3 * lax.rem(t, 2) if part else 2 - lax.rem(t, 2)
+                return lax.rem(z + step, 4), lax.rem(core + 1 - lax.div(t, 2), 2), 0
+
+            if part:
+                keep(u_out)
+            to_each(copy_to(u_out, False), order, 0, 4, part == 1)
+
+    def rows_by_core(u_first, u_second, u_out):
+        second = matrix(u_second)
+        act = copy_to(u_out, False)
+        for part in range(2):
+            wait_part(u_first, part)
+            own = lax.rem(core + 1 - part, 2)
+            planes = [own, own + 2]
+            both = jnp.concatenate([column_of(u_first, h) for h in planes], axis=1)
+            result = dot(both, second, 0, 0)
+            for k in range(2):
+                store_rows(u_out, planes[k], result[128 * k : 128 * k + 128])
+
+            def step(t, carry):
+                plane = own + 2 * lax.rem(t, 2)
+                core2 = lax.rem(core + 1 - lax.div(t, 2), 2)
+                for r_part, h_part in spots[:-1]:
+                    act(plane * 8 + r_part, core2 + h_part, 0)
+                r_part, h_part = spots[-1]
+
+                @pl.when(jnp.logical_or(plane != z, core2 != core))
+                def _():
+                    act(plane * 8 + r_part, core2 + h_part, 0)
+
+                return carry
+
+            lax.fori_loop(0, 4, step, 0)
+        keep(u_out)
+
+    def columns_by_core(u_first, u_second, u_out):
+        first = matrix(u_first)
+        for part in range(2):
+            wait_part(u_second, part)
+            own = lax.rem(core + 1 - part, 2)
+            columns = [own, own + 2]
+            both = jnp.concatenate([column_of(u_second, h) for h in columns], axis=1)
+            result = dot(first, both, 1, 0).astype(jnp.bfloat16)
+            for k in range(2):
+                block = result[:, 128 * k : 128 * k + 128]
+                snd[u_out, pl.ds(32 * columns[k], 32)] = block.reshape(32, 16, 128)
+            if part:
+                keep(u_out)
+            to_each(copy_to(u_out, False), by_core, 4 * part, 4, part == 1)
 
     def factor(layer, s, part, stage):
         both = dot(win_t[layer, 256 * part : 256 * part + 256, :], normed[s])
@@ -295,7 +383,7 @@
     prepare(1)
     whole(0).wait_recv()
     whole(1).wait_recv()
-    multiply(0, False, 1, True, 2)
+    multiply(0, 1, True, 2)
 
     fetch(2, stage_a)
 
@@ -309,21 +397,20 @@
         value = value.astype(jnp.bfloat16)
         held[1, s] = value
         input_norm(1, s, value.astype(jnp.float32))
-        factor(1, s, 0, stage_b)
+        factor(1, s, 1, stage_b)
 
     each_slab(middle)
-    flush(stage_b, 3)
-    each_slab(lambda s: factor(1, s, 1, stage_a))
-    flush(stage_a, 4)
+    flush(stage_b, 4)
+    each_slab(lambda s: factor(1, s, 0, stage_a))
+    flush(stage_a, 3, True)
 
     def rest_of_middle(s):
         open_gate(1, s)
         gtn[s] = mixed_back(1, s, upper[s].astype(jnp.float32))
 
     each_slab(rest_of_middle)
-    whole(3).wait_recv()
     whole(4).wait_recv()
-    multiply(3, True, 4, False, 5)
+    rows_by_core(3, 4, 5)
 
     fetch(5, stage_a)
 
@@ -333,7 +420,7 @@
         put(stage_b, s, normalise_back(gtn[s] * gain(1, 1), unit, inverse))
 
     each_slab(turn)
-    flush(stage_b, 6)
+    flush(stage_b, 6, True)
 
     def finish(s):
         mixed = dot(wout_t[1], tnorm[s])
@@ -345,35 +432,33 @@
         gate_back(1, s, upper[s].astype(jnp.float32), mixed)
 
     each_slab(finish)
-    whole(6).wait_recv()
-    multiply(4, False, 6, True, 7)
-    multiply(3, False, 6, False, 8)
-    fetch(7, stage_a)
-
-    def left_back(layer, s):
-        gnorm[s] = factor_back(layer, s, 0, stage_a)
-
-    each_slab(lambda s: left_back(1, s))
-    fetch(8, stage_b)
+    columns_by_core(3, 6, 8)
+    multiply(4, 6, True, 7)
+    fetch(8, stage_a)
+
+    def right_back(layer, s):
+        gnorm[s] = factor_back(layer, s, 1, stage_a)
+
+    each_slab(lambda s: right_back(1, s))
+    fetch(7, stage_b)
 
     def lower(s):
-        value = input_back(1, s, factor_back(1, s, 1, stage_b))
+        value = input_back(1, s, factor_back(1, s, 0, stage_b))
         upper[s] = value
         grad_tnorm = mixed_back(0, s, value.astype(jnp.float32))
         put(stage_a, s, normalise_back(grad_tnorm * gain(0, 1), unit_t[s], inv_t[s, 0:1, :]))
 
     each_slab(lower)
-    flush(stage_a, 9)
+    flush(stage_a, 9, True)
     each_slab(lambda s: gate_back(0, s, upper[s].astype(jnp.float32), mixed_s[s]))
-    whole(9).wait_recv()
-    multiply(9, False, 1, False, 10)
-    multiply(9, True, 0, False, 11)
-    fetch(10, stage_a)
-    each_slab(lambda s: left_back(0, s))
-    fetch(11, stage_b)
+    rows_by_core(9, 0, 11)
+    multiply(9, 1, False, 10)
+    fetch(11, stage_a)
+    each_slab(lambda s: right_back(0, s))
+    fetch(10, stage_b)
 
     def leave(s):
-        value = input_back(0, s, factor_back(0, s, 1, stage_b)).astype(jnp.float32)
+        value = input_back(0, s, factor_back(0, s, 0, stage_b)).astype(jnp.float32)
         for k in range(2):
             grad_ref[2 * s + k] = jnp.transpose(value[:, 128 * k : 128 * k + 128]).astype(
                 jnp.bfloat16
@@ -418,7 +503,7 @@
         pltpu.VMEM((UNITS, DEVICES, 16, 128), bf16),
         pltpu.VMEM((UNITS, DEVICES, 16, 128), bf16),
         pltpu.SemaphoreType.DMA((UNITS,)),
-        pltpu.SemaphoreType.DMA((UNITS,)),
+        pltpu.SemaphoreType.DMA((UNITS, 2)),
     ]
     shape = jax.ShapeDtypeStruct(pair_in.shape, bf16)
     return pl.pallas_call(

time: 115 us -> 113 us (0.983)
    pallas_call x1, Pallas kernels: 111 us -> 110 us  [local(): pl.pallas_call(kernel, out_shape=(shape, shape), in_specs=[vmem, vmem, sm...]
where the time goes in v4:
time: 113 us
  Pallas kernels  110 us (97%)
  local copies, waits for them, and re-layouts  2.74 us (2%)
    pallas_call x1, Pallas kernels, local(): pl.pallas_call(kernel, out_shape=(shape, shape), in_specs=[vmem, vmem, sm...  110 us
    unnamed x4, local copies, waits for them, and re-layouts  2.74 us

profile of v4, /device:TPU:1, one launch (start us, length us, event | category | flops | bytes accessed | tf_op | source)
XLA Modules:
  0.0 113.0 jit_solution(11009487070282735742)
XLA Ops:
  0.6 109.7 %shard_map.104 = (bf16[16,128,128]{2,1,0:T(8,128)(2,1)}, bf16[16,128,128]{2,1,0:T(8,128)(2,1)}) custom-call(bf16[16,128,128]{2,1,0:T(8,128)(2,1)} %pair_ref.1, bf16[16,128,128]{2,1,0:T(8,128)(2,1)} %gout_ref.1, s32[512]{0:T(512)} %valid_s.1, s32[512]{0:T(512)} %chain_s.1, s32[4,128]{1,0:T(4,128)} %bitcast.4, s32[4,128]{1,0:T(4,128)} %bitcast.5, ...), custom_call_target="tpu_custom_call" | custom-call | tf_op jit(solution)/shard_map/pallas_call | solution.py:509
  110.3 0.0 copy-start
  110.3 1.9 %copy.13 = bf16[16,128,128]{2,1,0:T(8,128)(2,1)} copy(bf16[16,128,128]{2,1,0:T(8,128)(2,1)} %get-tuple-element.4) | data formatting | bytes 1048576
  112.2 0.0 copy-done
  112.3 0.8 copy.14
Async XLA Ops:
  110.3 2.0 %copy-start = (bf16[16,128,128]{2,1,0:T(8,128)(2,1)S(1)}, bf16[16,128,128]{2,1,0:T(8,128)(2,1)}, u32[]{:S(2)}) copy-start(bf16[16,128,128]{2,1,0:T(8,128)(2,1)} %get-tuple-element.5) | copy-start | bytes 1572868

commit v5 on v4

--- a/solution.py
+++ b/solution.py
@@ -469,6 +469,11 @@
         whole(u).wait_send()
 
 
+def hand_over(first_in, second_in, first_out, second_out):
+    first_out[...] = first_in[...]
+    second_out[...] = second_in[...]
+
+
 def local(
     pair_in,
     grad_out,
@@ -506,7 +511,7 @@
         pltpu.SemaphoreType.DMA((UNITS, 2)),
     ]
     shape = jax.ShapeDtypeStruct(pair_in.shape, bf16)
-    return pl.pallas_call(
+    outs = pl.pallas_call(
         kernel,
         out_shape=(shape, shape),
         in_specs=[vmem, vmem, smem, smem] + [vmem] * 7,
@@ -528,6 +533,14 @@
         proj_in,
         proj_out,
     )
+    rows = pl.BlockSpec((8, 128, 128), lambda i: (i, 0, 0))
+    return pl.pallas_call(
+        hand_over,
+        out_shape=(shape, shape),
+        grid=(2,),
+        in_specs=[rows, rows],
+        out_specs=(rows, rows),
+    )(*outs)
 
 
 def solution(mesh):

time: 113 us -> 113 us (level)
  local copies, waits for them, and re-layouts: 2.74 us -> 0 us
  Pallas kernels: 110 us -> 112 us
    unnamed x4 -> x0, local copies, waits for them, and re-layouts: 2.74 us -> none
    pallas_call x0 -> x1, Pallas kernels: none -> 2.04 us  [local(): pl.pallas_call(hand_over, out_shape=(shape, shape), grid=(2,), in_specs=[...]
where the time goes in v5:
time: 113 us; the launch traced here: 112 us
  Pallas kernels  112 us (99%)
    pallas_call x1, Pallas kernels, local(): pl.pallas_call(kernel, out_shape=(shape, shape), in_specs=[vmem, vmem, sm...  110 us

profile of v5, /device:TPU:1, one launch (start us, length us, event | category | flops | bytes accessed | tf_op | source)
XLA Modules:
  0.0 112.3 jit_solution(10904614442175128046)
XLA Ops:
  0.6 109.7 %shard_map.104 = (bf16[16,128,128]{2,1,0:T(8,128)(2,1)}, bf16[16,128,128]{2,1,0:T(8,128)(2,1)}) custom-call(bf16[16,128,128]{2,1,0:T(8,128)(2,1)} %pair_ref.1, bf16[16,128,128]{2,1,0:T(8,128)(2,1)} %gout_ref.1, s32[512]{0:T(512)} %valid_s.1, s32[512]{0:T(512)} %chain_s.1, s32[4,128]{1,0:T(4,128)} %bitcast.4, s32[4,128]{1,0:T(4,128)} %bitcast.5, ...), custom_call_target="tpu_custom_call" | custom-call | tf_op jit(solution)/shard_map/pallas_call | solution.py:514
  110.3 2.0 %shard_map.105 = (bf16[16,128,128]{2,1,0:T(8,128)(2,1)}, bf16[16,128,128]{2,1,0:T(8,128)(2,1)}) custom-call(bf16[16,128,128]{2,1,0:T(8,128)(2,1)} %get-tuple-element.4.first_in, bf16[16,128,128]{2,1,0:T(8,128)(2,1)} %get-tuple-element.5.second_in), custom_call_target="tpu_custom_call" | custom-call | tf_op jit(solution)/shard_map/pallas_call | solution.py:537
